TPU v7x, 32 devices: a whole 2x2x4 slice. The times are simulated.
32 devices in a mesh: row: 8 (over z, x), col: 4 (over y, core).
Axes of the slice: x: 2, y: 2, z: 4, core: 2. Of those that a mesh axis runs over, the one named last changes fastest.
Arguments:
- object_field: float32 [2, 2048, 1024], P(None, 'row', 'col'), may hold values from -4.2 to 4.2
- probe_modes: float32 [2, 256, 512], P(None, 'row', 'col'), may hold values from -4.2 to 4.2
- measured: float32 [8, 4, 2, 256, 256], P('row', 'col'), may hold values from 0.3 to 3
- positions: int32 [8, 4, 2, 2], P('row', 'col'), may hold values from 0 to 128
- subset_order: int32 [8, 4, 2], P('row', 'col'), may hold values from 0 to 1, each once within a row
Outputs:
- object_out: float32 [2, 2048, 1024], P(None, 'row', 'col')
- probe_out: float32 [2, 256, 512], P(None, 'row', 'col')
Inputs may be any that keep to these rules, and one draw needn't show every extreme that they name: `positions`: A window of 256 pixels at these offsets lies inside the tile extended by 64 pixels on each side. `subset_order`: each tile's list is a permutation of its position numbers.
All inputs are finite; a program needn't handle non-finite values.
Results may differ from a plain program's by a relative error of at most 0.0017.
Values sent between devices are 32-bit elements; how exact they have to be, the bound alone decides.
A program may use at most 64 MiB of HBM per device.

v0:
```python
import math

import jax
import jax.numpy as jnp
from jax import lax
from jax.sharding import PartitionSpec as P

MARGIN = 64
SUBSETS = 2
OUTER = 2


amp_floor = 0.3
object_rate = 0.05


def extended_2(block, sides, width):
    for axis, dim in sides:
        count = lax.axis_size(axis)
        forward = [(i, i + 1) for i in range(count - 1)]
        backward = [(target, source) for source, target in forward]
        low = lax.ppermute(
            lax.slice_in_dim(block, block.shape[dim] - width, None, axis=dim), axis, forward
        )
        high = lax.ppermute(lax.slice_in_dim(block, 0, width, axis=dim), axis, backward)
        block = jnp.concatenate([low, block, high], axis=dim)
    return block


def tables(probe_size):
    ramp_values = jnp.arange(probe_size, dtype=jnp.int32)
    phases = ramp_values[:, None] * ramp_values[None, :] % probe_size
    angles = phases.astype(jnp.float32) * (2.0 * math.pi / probe_size)
    norming = 1.0 / math.sqrt(probe_size)
    cosine = jnp.cos(angles) * norming
    sine_part = jnp.sin(angles) * norming
    left_tables = jnp.stack([cosine, sine_part]).astype(jnp.bfloat16)
    right_forward = jnp.concatenate(
        [jnp.concatenate([cosine, -sine_part], 1), jnp.concatenate([sine_part, cosine], 1)], 0
    ).astype(jnp.bfloat16)
    right_inverse = jnp.concatenate(
        [jnp.concatenate([cosine, sine_part], 1), jnp.concatenate([-sine_part, cosine], 1)], 0
    ).astype(jnp.bfloat16)
    return (left_tables, right_forward, right_inverse)


def halves(values):
    middle = values.shape[-1] // 2
    return (values[..., :middle], values[..., middle:])


def multiply(former, latter, conjugate):
    former_re, former_im = halves(former)
    latter_re, latter_im = halves(latter)
    if conjugate:
        return jnp.concatenate(
            [
                former_re * latter_re + former_im * latter_im,
                former_re * latter_im - former_im * latter_re,
            ],
            -1,
        )
    return jnp.concatenate(
        [
            former_re * latter_re - former_im * latter_im,
            former_re * latter_im + former_im * latter_re,
        ],
        -1,
    )


def left_apply(left_tables, stacked, direction):
    products = jnp.einsum("tij,bjk->tbik", left_tables, stacked, preferred_element_type=jnp.float32)
    cos_re, cos_im = halves(products[0])
    sin_re, sin_im = halves(products[1])
    return jnp.concatenate([cos_re + direction * sin_im, cos_im - direction * sin_re], -1)


def project(windows, probe_full, amplitudes, left_tables, right_forward, right_inverse):
    exit_wave = multiply(probe_full[None], windows[:, None], False)
    count, mode_count, rows_here, cols_here = exit_wave.shape
    stacked = exit_wave.reshape(count * mode_count, rows_here, cols_here).astype(jnp.bfloat16)
    half_transform = left_apply(left_tables, stacked, 1.0).astype(jnp.bfloat16)
    far_field = jnp.einsum(
        "bik,kl->bil", half_transform, right_forward, preferred_element_type=jnp.float32
    )
    far_field = far_field.reshape(count, mode_count, rows_here, cols_here)
    far_re, far_im = halves(far_field)
    intensity = jnp.sum(far_re * far_re + far_im * far_im, axis=1)
    scaling = amplitudes / jnp.maximum(jnp.sqrt(intensity), amp_floor)
    scaling = jnp.concatenate([scaling, scaling], -1)[:, None]
    corrected = (
        (far_field * scaling).astype(jnp.bfloat16).reshape(count * mode_count, rows_here, cols_here)
    )
    returned = left_apply(left_tables, corrected, -1.0).astype(jnp.bfloat16)
    near_field = jnp.einsum(
        "bik,kl->bil", returned, right_inverse, preferred_element_type=jnp.float32
    )
    change = near_field.reshape(count, mode_count, rows_here, cols_here) - exit_wave
    window_gradient = jnp.sum(multiply(probe_full[None], change, True), axis=1)
    probe_gradient = jnp.sum(multiply(windows[:, None], change, True), axis=0)
    return (window_gradient, probe_gradient)


def spread(owned):
    gathered = lax.all_gather(owned, "col", axis=2, tiled=True)
    return lax.all_gather(gathered, "row", axis=1, tiled=True)


def fold(grad_extended, margin, tile_size):
    margins = jnp.concatenate(
        [grad_extended[:, :margin], grad_extended[:, tile_size + margin :]], 1
    )
    received = extended_2(margins, (("row", 1),), margin)
    interior = grad_extended[:, margin : margin + tile_size]
    interior = interior.at[:, :margin].add(received[:, :margin])
    interior = interior.at[:, tile_size - margin :].add(received[:, 3 * margin :])
    margins = jnp.concatenate([interior[:, :, :margin], interior[:, :, tile_size + margin :]], 2)
    received = extended_2(margins, (("col", 2),), margin)
    interior = interior[:, :, margin : margin + tile_size]
    interior = interior.at[:, :, :margin].add(received[:, :, :margin])
    interior = interior.at[:, :, tile_size - margin :].add(received[:, :, 3 * margin :])
    return interior


def shards(object_field, probe_modes, measured, positions, subset_order):
    probe_size = measured.shape[3]
    tile_size = object_field.shape[1]
    margin = MARGIN
    extent = tile_size + 2 * margin
    left_tables, right_forward, right_inverse = tables(probe_size)
    pos_count = subset_order.shape[2]
    subset_size = pos_count // SUBSETS
    probe_rate = 0.5 / (pos_count * lax.axis_size("row") * lax.axis_size("col"))
    probe_full = spread(probe_modes)
    for outer_step in range(OUTER):
        probe_total = jnp.zeros(probe_full.shape, jnp.float32)
        for subset in range(SUBSETS):
            extended = extended_2(object_field, (("row", 1), ("col", 2)), margin)
            chosen = subset_order[0, 0, subset * subset_size : (subset + 1) * subset_size]
            offsets = positions[0, 0][chosen]
            amplitudes = measured[0, 0][chosen]
            windows = []
            member = 0
            window_planes = lax.dynamic_slice(
                extended,
                (jnp.int32(0), offsets[member, 0], offsets[member, 1]),
                (2, probe_size, probe_size),
            )
            windows.append(jnp.concatenate([window_planes[0], window_planes[1]], -1))
            windows = jnp.stack(windows)
            window_gradient, probe_part = project(
                windows, probe_full, amplitudes, left_tables, right_forward, right_inverse
            )
            grad_extended = jnp.zeros((2, extent, extent), jnp.float32)
            member = 0
            grad_re, grad_im = halves(window_gradient[member])
            starts = (jnp.int32(0), offsets[member, 0], offsets[member, 1])
            grad_extended = lax.dynamic_update_slice(
                grad_extended, jnp.stack([grad_re, grad_im]), starts
            )
            object_field = object_field + object_rate * fold(grad_extended, margin, tile_size)
            probe_total = probe_total + probe_part
        owned_sum = lax.psum_scatter(probe_total, "row", scatter_dimension=1, tiled=True)
        owned_sum = lax.psum_scatter(owned_sum, "col", scatter_dimension=2, tiled=True)
        probe_modes = probe_modes + probe_rate * owned_sum
        if outer_step + 1 < OUTER:
            probe_full = spread(probe_modes)
    return (object_field, probe_modes)


def solution(mesh):
    in_specs = (
        P(None, "row", "col"),
        P(None, "row", "col"),
        P("row", "col", None, None, None),
        P("row", "col", None, None),
        P("row", "col", None),
    )
    out_specs = (P(None, "row", "col"), P(None, "row", "col"))
    return jax.shard_map(shards, mesh=mesh, in_specs=in_specs, out_specs=out_specs, check_vma=False)
```

profile of v0, /device:TPU:0, one launch (start us, length us, event | category | flops | bytes accessed | tf_op | source)
XLA Modules:
  0.0 515.7 jit_solution(4402169658525513013)
XLA Ops:
  8.3 4.8 collective-permute-start
  15.2 5.9 %all_gather.12 = f32[2,32,512]{2,0,1:T(2,128)} all-gather(f32[2,32,128]{2,0,1:T(2,128)S(1)} %copy.85), channel_id=1, replica_groups=mesh['row'=8,'col'=4] {'col'}, dimensions={2}, use_global_device_ids=true | all-gather | bytes 163840 | tf_op jit(solution)/shard_map/all_gather | solution.py:106
  40.2 23.7 %all-gather.3.cloned.1.call-done = f32[2,256,512]{2,0,1:T(2,128)} async-done(((f32[2,32,512]{2,0,1:T(2,128)}), f32[2,256,512]{2,0,1:T(2,128)}) %all-gather.3.cloned.1.call-update) | async-done | bytes 1048592 | tf_op jit(solution)/shard_map/all_gather | solution.py:107
  73.6 7.1 %dynamic_update_slice.12 = f32[2,384,384]{2,1,0:T(8,128)S(1)} dynamic-update-slice(f32[2,384,384]{2,1,0:T(8,128)S(1)} %broadcast.373.clone, f32[2,256,256]{2,1,0:T(8,128)S(1)} %copy-done.6, s32[]{:T(128)} %constant.370.clone.1, s32[]{:T(128)S(6)} %select_n.73, s32[]{:T(128)S(6)} %select_n.74) | dynamic-update-slice | bytes 1048580 | tf_op jit(solution)/shard_map/dynamic_update_slice | solution.py:159
  106.8 4.9 collective-permute-done.9
  111.9 5.5 %collective-permute-start.10 = (f32[2,384,64]{2,1,0:T(8,128)S(1)}, f32[2,384,64]{2,1,0:T(8,128)S(1)}, u32[]{:S(2)}, u32[]{:S(2)}) collective-permute-start(f32[2,384,64]{2,1,0:T(8,128)S(1)} %get-tuple-element.335), channel_id=1, source_target_pairs={{0,1},{1,2},{2,3},{4,5},{5,6},{6,7},{8,9},{9,10},{10,11},{12,13},{... | collective-permute-start | bytes 589832 | tf_op jit(solution)/shard_map/ppermute | solution.py:22
  132.6 8.0 %dynamic_update_slice.13 = f32[2,384,384]{2,1,0:T(8,128)S(1)} dynamic-update-slice(f32[2,384,384]{2,1,0:T(8,128)S(1)} %broadcast.373.clone.1, f32[2,256,256]{2,1,0:T(8,128)S(1)} %copy.104, s32[]{:T(128)} %constant.370.clone.1, s32[]{:T(128)S(6)} %select_n.78, s32[]{:T(128)S(6)} %select_n.79) | dynamic-update-slice | bytes 1048580 | tf_op jit(solution)/shard_map/dynamic_update_slice | solution.py:159
  152.9 6.1 %collective-permute-start.14 = (f32[2,256,64]{2,1,0:T(8,128)S(1)}, f32[2,256,64]{2,1,0:T(8,128)S(1)}, u32[]{:S(2)}, u32[]{:S(2)}) collective-permute-start(f32[2,256,64]{2,1,0:T(8,128)S(1)} %get-tuple-element.333), channel_id=1, source_target_pairs={{0,1},{1,2},{2,3},{4,5},{5,6},{6,7},{8,9},{9,10},{10,11},{12,13},{... | collective-permute-start | bytes 393224 | tf_op jit(solution)/shard_map/ppermute | solution.py:22
  161.8 55.9 %all-reduce.5.cloned.1.call-done = f32[2,256,512]{2,0,1:T(2,128)} async-done(((f32[2,256,512]{2,0,1:T(2,128)}), f32[2,256,512]{2,0,1:T(2,128)}) %all-reduce.5.cloned.1.call-update) | async-done | bytes 1048592
  218.6 7.6 %copy.157 = f32[2,32,512]{0,1,2:T(8,128)} copy(f32[2,32,512]{2,0,1:T(2,128)S(1)} %constant_dynamic-slice_fusion.3) | data formatting | bytes 262144
  226.2 8.8 %reshape.822 = f32[512,64]{1,0:T(8,128)} reshape(f32[512,32,2]{2,1,0:T(8,128)} %bitcast.258) | data formatting | bytes 262144
  238.1 16.7 %reduce-scatter.7.cloned.1.call-done = f32[128,64]{1,0:T(8,128)} async-done(((f32[512,64]{1,0:T(8,128)}), f32[128,64]{1,0:T(8,128)}) %reduce-scatter.7.cloned.1.call-update) | async-done | bytes 32784
  259.2 5.9 %all_gather.14 = f32[2,32,512]{2,0,1:T(2,128)} all-gather(f32[2,32,128]{2,0,1:T(2,128)S(1)} %multiply_add_fusion.17), channel_id=1, replica_groups=mesh['row'=8,'col'=4] {'col'}, dimensions={2}, use_global_device_ids=true | all-gather | bytes 163840 | tf_op jit(solution)/shard_map/all_gather | solution.py:106
  283.1 22.6 %all-gather.5.cloned.1.call-done = f32[2,256,512]{2,0,1:T(2,128)} async-done(((f32[2,32,512]{2,0,1:T(2,128)}), f32[2,256,512]{2,0,1:T(2,128)}) %all-gather.5.cloned.1.call-update) | async-done | bytes 1048592 | tf_op jit(solution)/shard_map/all_gather | solution.py:107
  313.6 7.2 %dynamic_update_slice.14 = f32[2,384,384]{2,1,0:T(8,128)S(1)} dynamic-update-slice(f32[2,384,384]{2,1,0:T(8,128)S(1)} %broadcast.373.clone.2, f32[2,256,256]{2,1,0:T(8,128)S(1)} %copy.116, s32[]{:T(128)} %constant.370.clone.1, s32[]{:T(128)S(6)} %select_n.73, s32[]{:T(128)S(6)} %select_n.74) | dynamic-update-slice | bytes 1048580 | tf_op jit(solution)/shard_map/dynamic_update_slice | solution.py:159
  346.8 4.9 collective-permute-done.25
  351.9 5.5 %collective-permute-start.26 = (f32[2,384,64]{2,1,0:T(8,128)S(1)}, f32[2,384,64]{2,1,0:T(8,128)S(1)}, u32[]{:S(2)}, u32[]{:S(2)}) collective-permute-start(f32[2,384,64]{2,1,0:T(8,128)S(1)} %get-tuple-element.327), channel_id=1, source_target_pairs={{0,1},{1,2},{2,3},{4,5},{5,6},{6,7},{8,9},{9,10},{10,11},{12,13},{... | collective-permute-start | bytes 589832 | tf_op jit(solution)/shard_map/ppermute | solution.py:22
  368.9 8.0 %dynamic_update_slice.15 = f32[2,384,384]{2,1,0:T(8,128)S(1)} dynamic-update-slice(f32[2,384,384]{2,1,0:T(8,128)S(1)} %broadcast.373, f32[2,256,256]{2,1,0:T(8,128)S(1)} %copy.125, s32[]{:T(128)} %constant.370.clone.1, s32[]{:T(128)S(6)} %select_n.78, s32[]{:T(128)S(6)} %select_n.79) | dynamic-update-slice | bytes 1048580 | tf_op jit(solution)/shard_map/dynamic_update_slice | solution.py:159
  387.3 6.2 %collective-permute-done.29 = f32[2,64,384]{2,1,0:T(8,128)S(1)} collective-permute-done((f32[2,64,384]{2,1,0:T(8,128)S(1)}, f32[2,64,384]{2,1,0:T(8,128)S(1)}, u32[]{:S(2)}, u32[]{:S(2)}) %collective-permute-start.29) | collective-permute-done | bytes 196640 | tf_op jit(solution)/shard_map/ppermute | solution.py:25
  393.7 9.9 %collective-permute-start.30 = (f32[2,256,64]{2,1,0:T(8,128)S(1)}, f32[2,256,64]{2,1,0:T(8,128)S(1)}, u32[]{:S(2)}, u32[]{:S(2)}) collective-permute-start(f32[2,256,64]{2,1,0:T(8,128)S(1)} %get-tuple-element.325), channel_id=1, source_target_pairs={{0,1},{1,2},{2,3},{4,5},{5,6},{6,7},{8,9},{9,10},{10,11},{12,13},{... | collective-permute-start | bytes 393224 | tf_op jit(solution)/shard_map/ppermute | solution.py:22
  409.4 57.1 %all-reduce.7.cloned.1.call-done = f32[2,256,512]{2,0,1:T(2,128)} async-done(((f32[2,256,512]{2,0,1:T(2,128)}), f32[2,256,512]{2,0,1:T(2,128)}) %all-reduce.7.cloned.1.call-update) | async-done | bytes 1048592
  467.4 7.6 %copy.159 = f32[2,32,512]{0,1,2:T(8,128)} copy(f32[2,32,512]{2,0,1:T(2,128)S(1)} %constant_dynamic-slice_fusion.2) | data formatting | bytes 262144
  475.0 8.8 %reshape.824 = f32[512,64]{1,0:T(8,128)} reshape(f32[512,32,2]{2,1,0:T(8,128)} %bitcast.259) | data formatting | bytes 262144
  484.7 18.9 %reduce-scatter.9.cloned.1.call-done = f32[128,64]{1,0:T(8,128)} async-done(((f32[512,64]{1,0:T(8,128)}), f32[128,64]{1,0:T(8,128)}) %reduce-scatter.9.cloned.1.call-update) | async-done | bytes 32784
  (303 shorter events, 170.2 us)
Async XLA Ops:
  7.2 56.7 %all-gather.3.cloned.1.call-start = ((), (), s32[]{:S(2)}) async-start(), calls=%async_computation.2 | async-start | bytes 1179648 | tf_op jit(solution)/shard_map/all_gather | solution.py:107
  8.3 24.2 %collective-permute-start = (f32[2,64,256]{2,1,0:T(8,128)S(1)}, f32[2,64,256]{2,1,0:T(8,128)S(1)}, u32[]{:S(2)}, u32[]{:S(2)}) collective-permute-start(f32[2,64,256]{2,1,0:T(8,128)S(1)} %get-tuple-element.371), channel_id=1, source_target_pairs={{0,4},{4,8},{8,12},{12,16},{16,20},{20,24},{24,28},{1,5},{5,9},{9,... | collective-permute-start | bytes 393224 | tf_op jit(solution)/shard_map/ppermute | solution.py:22
  13.1 19.4 %collective-permute-start.1 = (f32[2,64,256]{2,1,0:T(8,128)S(1)}, f32[2,64,256]{2,1,0:T(8,128)S(1)}, u32[]{:S(2)}, u32[]{:S(2)}) collective-permute-start(f32[2,64,256]{2,1,0:T(8,128)S(1)} %get-tuple-element.370), channel_id=1, source_target_pairs={{4,0},{8,4},{12,8},{16,12},{20,16},{24,20},{28,24},{5,1},{9,5},{13... | collective-permute-start | bytes 393224 | tf_op jit(solution)/shard_map/ppermute | solution.py:25
  21.1 196.6 %all-reduce.5.cloned.1.call-start = ((), (), s32[]{:S(2)}) async-start(), calls=%async_computation.6 | async-start | bytes 2097152
  83.3 7.6 %collective-permute-start.5 = (f32[2,64,384]{2,1,0:T(8,128)S(1)}, f32[2,64,384]{2,1,0:T(8,128)S(1)}, u32[]{:S(2)}, u32[]{:S(2)}) collective-permute-start(f32[2,64,384]{2,1,0:T(8,128)S(1)} %get-tuple-element.314), channel_id=1, source_target_pairs={{4,0},{8,4},{12,8},{16,12},{20,16},{24,20},{28,24},{5,1},{9,5},{13... | collective-permute-start | bytes 589832 | tf_op jit(solution)/shard_map/ppermute | solution.py:25
  100.0 6.7 %collective-permute-start.8 = (f32[2,64,256]{2,1,0:T(8,128)S(1)}, f32[2,64,256]{2,1,0:T(8,128)S(1)}, u32[]{:S(2)}, u32[]{:S(2)}) collective-permute-start(f32[2,64,256]{2,1,0:T(8,128)S(1)} %get-tuple-element.362), channel_id=1, source_target_pairs={{0,4},{4,8},{8,12},{12,16},{16,20},{20,24},{24,28},{1,5},{5,9},{9,... | collective-permute-start | bytes 393224 | tf_op jit(solution)/shard_map/ppermute | solution.py:22
  104.3 7.4 %collective-permute-start.9 = (f32[2,64,256]{2,1,0:T(8,128)S(1)}, f32[2,64,256]{2,1,0:T(8,128)S(1)}, u32[]{:S(2)}, u32[]{:S(2)}) collective-permute-start(f32[2,64,256]{2,1,0:T(8,128)S(1)} %get-tuple-element.363), channel_id=1, source_target_pairs={{4,0},{8,4},{12,8},{16,12},{20,16},{24,20},{28,24},{5,1},{9,5},{13... | collective-permute-start | bytes 393224 | tf_op jit(solution)/shard_map/ppermute | solution.py:25
  111.9 10.7 %collective-permute-start.10 = (f32[2,384,64]{2,1,0:T(8,128)S(1)}, f32[2,384,64]{2,1,0:T(8,128)S(1)}, u32[]{:S(2)}, u32[]{:S(2)}) collective-permute-start(f32[2,384,64]{2,1,0:T(8,128)S(1)} %get-tuple-element.335), channel_id=1, source_target_pairs={{0,1},{1,2},{2,3},{4,5},{5,6},{6,7},{8,9},{9,10},{10,11},{12,13},{... | collective-permute-start | bytes 589832 | tf_op jit(solution)/shard_map/ppermute | solution.py:22
  132.1 122.8 %reduce-scatter.7.cloned.1.call-start = ((), (), s32[]{:S(2)}) async-start(), calls=%async_computation.4 | async-start | bytes 327680
  140.6 7.6 %collective-permute-start.12 = (f32[2,64,384]{2,1,0:T(8,128)S(1)}, f32[2,64,384]{2,1,0:T(8,128)S(1)}, u32[]{:S(2)}, u32[]{:S(2)}) collective-permute-start(f32[2,64,384]{2,1,0:T(8,128)S(1)} %get-tuple-element.313), channel_id=1, source_target_pairs={{0,4},{4,8},{8,12},{12,16},{16,20},{20,24},{24,28},{1,5},{5,9},{9,... | collective-permute-start | bytes 589832 | tf_op jit(solution)/shard_map/ppermute | solution.py:22
  145.1 7.6 %collective-permute-start.13 = (f32[2,64,384]{2,1,0:T(8,128)S(1)}, f32[2,64,384]{2,1,0:T(8,128)S(1)}, u32[]{:S(2)}, u32[]{:S(2)}) collective-permute-start(f32[2,64,384]{2,1,0:T(8,128)S(1)} %get-tuple-element.312), channel_id=1, source_target_pairs={{4,0},{8,4},{12,8},{16,12},{20,16},{24,20},{28,24},{5,1},{9,5},{13... | collective-permute-start | bytes 589832 | tf_op jit(solution)/shard_map/ppermute | solution.py:25
  152.9 82.6 %collective-permute-start.14 = (f32[2,256,64]{2,1,0:T(8,128)S(1)}, f32[2,256,64]{2,1,0:T(8,128)S(1)}, u32[]{:S(2)}, u32[]{:S(2)}) collective-permute-start(f32[2,256,64]{2,1,0:T(8,128)S(1)} %get-tuple-element.333), channel_id=1, source_target_pairs={{0,1},{1,2},{2,3},{4,5},{5,6},{6,7},{8,9},{9,10},{10,11},{12,13},{... | collective-permute-start | bytes 393224 | tf_op jit(solution)/shard_map/ppermute | solution.py:22
  160.5 76.3 %collective-permute-start.15 = (f32[2,256,64]{2,1,0:T(8,128)S(1)}, f32[2,256,64]{2,1,0:T(8,128)S(1)}, u32[]{:S(2)}, u32[]{:S(2)}) collective-permute-start(f32[2,256,64]{2,1,0:T(8,128)S(1)} %get-tuple-element.332), channel_id=1, source_target_pairs={{1,0},{2,1},{3,2},{5,4},{6,5},{7,6},{9,8},{10,9},{11,10},{13,12},{... | collective-permute-start | bytes 393224 | tf_op jit(solution)/shard_map/ppermute | solution.py:25
  235.0 70.6 %all-gather.5.cloned.1.call-start = ((), (), s32[]{:S(2)}) async-start(), calls=%async_computation.3 | async-start | bytes 1179648 | tf_op jit(solution)/shard_map/all_gather | solution.py:107
  265.2 201.3 %all-reduce.7.cloned.1.call-start = ((), (), s32[]{:S(2)}) async-start(), calls=%async_computation.7 | async-start | bytes 2097152
  268.7 7.5 %collective-permute-start.17 = (f32[2,64,256]{2,1,0:T(8,128)S(1)}, f32[2,64,256]{2,1,0:T(8,128)S(1)}, u32[]{:S(2)}, u32[]{:S(2)}) collective-permute-start(f32[2,64,256]{2,1,0:T(8,128)S(1)} %get-tuple-element.355), channel_id=1, source_target_pairs={{4,0},{8,4},{12,8},{16,12},{20,16},{24,20},{28,24},{5,1},{9,5},{13... | collective-permute-start | bytes 393224 | tf_op jit(solution)/shard_map/ppermute | solution.py:25
  323.4 7.6 %collective-permute-start.21 = (f32[2,64,384]{2,1,0:T(8,128)S(1)}, f32[2,64,384]{2,1,0:T(8,128)S(1)}, u32[]{:S(2)}, u32[]{:S(2)}) collective-permute-start(f32[2,64,384]{2,1,0:T(8,128)S(1)} %get-tuple-element.310), channel_id=1, source_target_pairs={{4,0},{8,4},{12,8},{16,12},{20,16},{24,20},{28,24},{5,1},{9,5},{13... | collective-permute-start | bytes 589832 | tf_op jit(solution)/shard_map/ppermute | solution.py:25
  340.1 6.8 %collective-permute-start.24 = (f32[2,64,256]{2,1,0:T(8,128)S(1)}, f32[2,64,256]{2,1,0:T(8,128)S(1)}, u32[]{:S(2)}, u32[]{:S(2)}) collective-permute-start(f32[2,64,256]{2,1,0:T(8,128)S(1)} %get-tuple-element.346), channel_id=1, source_target_pairs={{0,4},{4,8},{8,12},{12,16},{16,20},{20,24},{24,28},{1,5},{5,9},{9,... | collective-permute-start | bytes 393224 | tf_op jit(solution)/shard_map/ppermute | solution.py:22
  344.3 7.4 %collective-permute-start.25 = (f32[2,64,256]{2,1,0:T(8,128)S(1)}, f32[2,64,256]{2,1,0:T(8,128)S(1)}, u32[]{:S(2)}, u32[]{:S(2)}) collective-permute-start(f32[2,64,256]{2,1,0:T(8,128)S(1)} %get-tuple-element.347), channel_id=1, source_target_pairs={{4,0},{8,4},{12,8},{16,12},{20,16},{24,20},{28,24},{5,1},{9,5},{13... | collective-permute-start | bytes 393224 | tf_op jit(solution)/shard_map/ppermute | solution.py:25
  351.9 6.9 %collective-permute-start.26 = (f32[2,384,64]{2,1,0:T(8,128)S(1)}, f32[2,384,64]{2,1,0:T(8,128)S(1)}, u32[]{:S(2)}, u32[]{:S(2)}) collective-permute-start(f32[2,384,64]{2,1,0:T(8,128)S(1)} %get-tuple-element.327), channel_id=1, source_target_pairs={{0,1},{1,2},{2,3},{4,5},{5,6},{6,7},{8,9},{9,10},{10,11},{12,13},{... | collective-permute-start | bytes 589832 | tf_op jit(solution)/shard_map/ppermute | solution.py:22
  377.7 9.5 %collective-permute-start.28 = (f32[2,64,384]{2,1,0:T(8,128)}, f32[2,64,384]{2,1,0:T(8,128)S(1)}, u32[]{:S(2)}, u32[]{:S(2)}) collective-permute-start(f32[2,64,384]{2,1,0:T(8,128)} %get-tuple-element.309), channel_id=1, source_target_pairs={{0,4},{4,8},{8,12},{12,16},{16,20},{20,24},{24,28},{1,5},{5,9},{9,... | collective-permute-start | bytes 589832 | tf_op jit(solution)/shard_map/ppermute | solution.py:22
  385.9 117.7 %reduce-scatter.9.cloned.1.call-start = ((), (), s32[]{:S(2)}) async-start(), calls=%async_computation.5 | async-start | bytes 327680
  385.9 7.6 %collective-permute-start.29 = (f32[2,64,384]{2,1,0:T(8,128)S(1)}, f32[2,64,384]{2,1,0:T(8,128)S(1)}, u32[]{:S(2)}, u32[]{:S(2)}) collective-permute-start(f32[2,64,384]{2,1,0:T(8,128)S(1)} %get-tuple-element.308), channel_id=1, source_target_pairs={{4,0},{8,4},{12,8},{16,12},{20,16},{24,20},{28,24},{5,1},{9,5},{13... | collective-permute-start | bytes 589832 | tf_op jit(solution)/shard_map/ppermute | solution.py:25
  393.7 11.6 %collective-permute-start.30 = (f32[2,256,64]{2,1,0:T(8,128)S(1)}, f32[2,256,64]{2,1,0:T(8,128)S(1)}, u32[]{:S(2)}, u32[]{:S(2)}) collective-permute-start(f32[2,256,64]{2,1,0:T(8,128)S(1)} %get-tuple-element.325), channel_id=1, source_target_pairs={{0,1},{1,2},{2,3},{4,5},{5,6},{6,7},{8,9},{9,10},{10,11},{12,13},{... | collective-permute-start | bytes 393224 | tf_op jit(solution)/shard_map/ppermute | solution.py:22
  (43 other events, 236.2 us)
Sparse Core Ops, SparseCore 0:
  21.3 42.5 all-gather.2
  132.2 85.4 all-reduce.4
  235.2 19.6 reduce-scatter.6
  265.3 40.2 all-gather.4
  386.0 80.4 all-reduce.6
  484.0 19.6 reduce-scatter.8
where the time goes:
time: 524 us; the launch traced here: 516 us
  waiting for transfers between devices  253 us (48%)
  local copies, waits for them, and re-layouts  111 us (21%)
  starting transfers between devices  86.1 us (16%)
  between operations  27.7 us (5%)
  other arithmetic  17.9 us (3%)
  blocking collectives  11.8 us (2%)
  matrix products  7.64 us (1%)
    unnamed x10, waiting for transfers between devices  149 us
    ppermute x16, starting transfers between devices, extended_2(): lax.ppermute(lax.slice_in_dim(block, block.shape[dim] - width, None, axis...  64.2 us
    unnamed x73, local copies, waits for them, and re-layouts  54.2 us
    ppermute x16, waiting for transfers between devices, extended_2(): lax.ppermute(lax.slice_in_dim(block, 0, width, axis=dim), axis, backward)  48.3 us
    all_gather x2, waiting for transfers between devices, spread(): return lax.all_gather(gathered, 'row', axis=1, tiled=True)  46.2 us
    dynamic_update_slice x4, local copies, waits for them, and re-layouts, shards(): lax.dynamic_update_slice(grad_extended, jnp.stack([grad_re, grad_im]), st...  30.4 us
    ppermute x16, starting transfers between devices, extended_2(): lax.ppermute(lax.slice_in_dim(block, 0, width, axis=dim), axis, backward)  21.3 us
    all_gather x2, blocking collectives, spread(): gathered = lax.all_gather(owned, 'col', axis=2, tiled=True)  11.8 us
  transfers between devices with their start and end apart: 38, of which 25 were waited for; matrix products, arithmetic and copies ran while one was open for 9% of the time, Pallas kernels for 0%

commit v1 on v0

--- a/solution.py
+++ b/solution.py
@@ -1,8 +1,13 @@
+import functools
 import math
 
 import jax
 import jax.numpy as jnp
+import ml_dtypes
+import numpy as np
 from jax import lax
+from jax.experimental import pallas as pl
+from jax.experimental.pallas import tpu as pltpu
 from jax.sharding import PartitionSpec as P
 
 MARGIN = 64
@@ -169,6 +174,618 @@
     return (object_field, probe_modes)
 
 
+LANES = 128
+
+
+def host_tables(probe_size):
+    ramp_values = np.arange(probe_size, dtype=np.int32)
+    phases = ramp_values[:, None] * ramp_values[None, :] % probe_size
+    angles = phases.astype(np.float32) * np.float32(2.0 * math.pi / probe_size)
+    norming = np.float32(1.0 / math.sqrt(probe_size))
+    cosine = np.cos(angles) * norming
+    sine_part = np.sin(angles) * norming
+    left_tables = np.stack([cosine, sine_part]).astype(ml_dtypes.bfloat16)
+    right_forward = np.block([[cosine, -sine_part], [sine_part, cosine]]).astype(ml_dtypes.bfloat16)
+    right_inverse = np.block([[cosine, sine_part], [-sine_part, cosine]]).astype(ml_dtypes.bfloat16)
+    return (left_tables, right_forward, right_inverse)
+
+
+def kernel(
+    n_row, n_col, probe_rate,
+    pos_ref, order_ref, obj_ref, prb_ref, meas_ref, lt_ref, rf_ref, ri_ref,
+    out_obj, out_prb,
+    ext, acc, gpad, win, ew, xb, zb, offs, roffs, srow, rrow, rcol,
+    pf, pg, hs, rc, ry, ss, rr, ssem, rsem,
+):
+    r = lax.axis_index("row")
+    c = lax.axis_index("col")
+    tile = obj_ref.shape[1]
+    width = meas_ref.shape[1]
+    modes, pr, pw = prb_ref.shape
+    margin = MARGIN
+    strip = 2 * margin
+    extent = tile + strip
+    passes = OUTER * SUBSETS
+    half = n_col // 2
+    core = lax.rem(c, 2)
+    q = lax.div(c, 2)
+    sibling = c + 1 - 2 * core
+    block = strip
+    blocks = width // block
+    pieces = block // pr
+    f32 = jnp.float32
+    ids = {}
+
+    def sem_id(key):
+        return ids.setdefault(key, len(ids))
+
+    def copy(key, src, dst, device):
+        index = sem_id(key)
+        return pltpu.make_async_remote_copy(
+            src_ref=src, dst_ref=dst, send_sem=ssem.at[index], recv_sem=rsem.at[index],
+            device_id=device, device_id_type=pl.DeviceIdType.MESH,
+        )
+
+    barrier = pltpu.get_barrier_semaphore()
+    for step in range(1, n_row):
+        pl.semaphore_signal(
+            barrier, inc=1, device_id=(lax.rem(r + step, n_row), c),
+            device_id_type=pl.DeviceIdType.MESH,
+        )
+    for step in range(1, n_col):
+        pl.semaphore_signal(
+            barrier, inc=1, device_id=(r, lax.rem(c + step, n_col)),
+            device_id_type=pl.DeviceIdType.MESH,
+        )
+    pl.semaphore_wait(barrier, n_row - 1 + n_col - 1)
+
+    has_up, has_down = r > 0, r < n_row - 1
+    has_left, has_right = c > 0, c < n_col - 1
+    lanes = lax.broadcasted_iota(jnp.int32, (block, LANES), 1)
+
+
+    def row_copy(e, side):
+        if e == 0:
+            rows = pl.ds(0, margin)
+            src = obj_ref.at[:, pl.ds(0, margin)] if side == 0 else obj_ref.at[:, pl.ds(tile - margin, margin)]
+        elif e == passes:
+            rows = pl.ds(0, margin)
+            src = srow.at[side, :, rows]
+        else:
+            src = srow.at[side]
+            rows = pl.ds(0, strip)
+        dst = rrow.at[e, 1 - side, :, rows]
+        return copy(("row", e, side), src, dst, (r - 1 if side == 0 else r + 1, c))
+
+    def col_copy(e, side, part):
+        low, size = [(0, strip), (strip, tile - strip), (tile, strip)][part]
+        if e == passes:
+            low, size = [(margin, margin), (strip, tile - strip), (tile, margin)][part]
+        rows = pl.ds(low, size)
+        src = acc.at[2 * side, :, rows]
+        dst = rcol.at[e, 1 - side, :, rows]
+        return copy(("col", e, side, part), src, dst, (r, c - 1 if side == 0 else c + 1))
+
+    def off_copy(side):
+        return copy(("off", side), offs, roffs.at[1 - side], (r - 1 if side == 0 else r + 1, c))
+
+    def start_cols(e, part):
+        @pl.when(has_left)
+        def _():
+            col_copy(e, 0, part).start()
+
+        @pl.when(has_right)
+        def _():
+            col_copy(e, 1, part).start()
+
+
+    def ag_row(g, step):
+        return copy(
+            ("agr", g, step), pf.at[g, c, r], pf.at[g, c, r], (lax.rem(r + step, n_row), c)
+        )
+
+    def ag_sib(g, step):
+        at = lax.rem(r + n_row - step, n_row)
+        return copy(("ags", g, step), pf.at[g, c, at], pf.at[g, c, at], (r, sibling))
+
+    def ag_par(g, step, other):
+        at = lax.rem(r + n_row - step, n_row)
+        to = 2 * lax.rem(q + other, half) + core
+        return copy(("agp", g, step, other), pf.at[g, c, at], pf.at[g, c, at], (r, to))
+
+    def ag_fwd(g, step, other):
+        at = lax.rem(r + n_row - step, n_row)
+        held = 2 * lax.rem(q + half - other, half) + core
+        return copy(("agf", g, step, other), pf.at[g, held, at], pf.at[g, held, at], (r, sibling))
+
+    def gather_send(g):
+        for step in range(1, n_row):
+            ag_row(g, step).start()
+        ag_sib(g, 0).start()
+        for other in range(1, half):
+            ag_par(g, 0, other).start()
+
+    def gather_pass_on(g):
+        for step in range(1, n_row):
+            ag_row(g, step).wait_recv()
+            for other in range(1, half):
+                ag_par(g, step, other).start()
+            ag_sib(g, step).start()
+        for step in range(n_row):
+            for other in range(1, half):
+                ag_par(g, step, other).wait_recv()
+                ag_fwd(g, step, other).start()
+
+    def gather_end(g):
+        for step in range(n_row):
+            ag_sib(g, step).wait_recv()
+            for other in range(1, half):
+                ag_fwd(g, step, other).wait_recv()
+        for step in range(n_row):
+            if step:
+                ag_row(g, step).wait_send()
+            ag_sib(g, step).wait_send()
+            for other in range(1, half):
+                ag_par(g, step, other).wait_send()
+                ag_fwd(g, step, other).wait_send()
+
+
+    def rs_core(t, k):
+        return copy(("rsc", t, k), pg.at[2 * k + 1 - core], rc.at[t, k], (r, sibling))
+
+    def rs_par(t, step, other):
+        at = lax.rem(r + step, n_row)
+        to_q = lax.rem(q + other, half)
+        return copy(
+            ("rsp", t, step, other), hs.at[to_q, at], ry.at[t, other, at], (r, 2 * to_q + core)
+        )
+
+    def rs_row(t, step):
+        at = lax.rem(r + step, n_row)
+        return copy(("rsr", t, step), ss.at[step], rr.at[t, step], (at, c))
+
+    def sum_start(t):
+        for k in range(half):
+            rs_core(t, k).start()
+
+    order = list(range(1, n_row)) + [0]
+
+    def sum_pass_on(t):
+        for k in range(half):
+            rs_core(t, k).wait_recv()
+        for step in order:
+            at = lax.rem(r + step, n_row)
+            for other in range(1, half):
+                to_q = lax.rem(q + other, half)
+                hs[to_q, at] = pg[2 * to_q + core, at] + rc[t, to_q, at]
+                rs_par(t, step, other).start()
+        for step in order:
+            at = lax.rem(r + step, n_row)
+            value = pg[c, at] + rc[t, q, at]
+            for other in range(1, half):
+                rs_par(t, step, other).wait_recv()
+                value = value + ry[t, other, at]
+            ss[step] = value
+            if step:
+                rs_row(t, step).start()
+
+    def sum_end(t):
+        value = ss[0]
+        for step in range(1, n_row):
+            rs_row(t, step).wait_recv()
+            value = value + rr[t, step]
+        return value
+
+    def sum_sent(t):
+        for k in range(half):
+            rs_core(t, k).wait_send()
+        for step in range(n_row):
+            for other in range(1, half):
+                rs_par(t, step, other).wait_send()
+            if step:
+                rs_row(t, step).wait_send()
+
+
+    for subset in range(SUBSETS):
+        offs[subset] = jnp.full(offs.shape[1:], pos_ref[order_ref[subset], 1], jnp.int32)
+
+    @pl.when(has_up)
+    def _():
+        row_copy(0, 0).start()
+        off_copy(0).start()
+
+    @pl.when(has_down)
+    def _():
+        row_copy(0, 1).start()
+        off_copy(1).start()
+
+    pf[0, c, r] = prb_ref[...]
+    gather_send(0)
+
+    def placed(values):
+        rows = values.shape[0]
+        spot = lax.broadcasted_iota(jnp.int32, (rows, LANES), 1) >= margin
+        first = pltpu.roll(values[:, :LANES], margin, 1)
+        second = pltpu.roll(values[:, LANES:], margin, 1)
+        zero = jnp.zeros_like(first)
+        return (
+            jnp.where(spot, first, zero), jnp.where(spot, second, first),
+            jnp.where(spot, zero, second),
+        )
+
+    for plane in range(2):
+        for k in range(2):
+            gpad[plane, k, 0:strip] = jnp.zeros((strip, LANES), f32)
+            gpad[plane, k, strip + width :] = jnp.zeros((strip, LANES), f32)
+        for low in range(0, tile, margin):
+            parts = placed(obj_ref[plane, low : low + margin])
+            for b in range(3):
+                acc[b, plane, margin + low : 2 * margin + low] = parts[b]
+    start_cols(0, 1)
+
+    def halo_rows(side, at):
+        for plane in range(2):
+            parts = placed(rrow[0, side, plane, 0:margin])
+            for b in range(3):
+                acc[b, plane, at : at + margin] = parts[b]
+
+    def halo_zero(at):
+        for plane in range(2):
+            for b in range(3):
+                acc[b, plane, at : at + margin] = jnp.zeros((margin, LANES), f32)
+
+    @pl.when(has_down)
+    def _():
+        row_copy(0, 0).wait_recv()
+        off_copy(0).wait_recv()
+        halo_rows(1, tile + margin)
+
+    @pl.when(jnp.logical_not(has_down))
+    def _():
+        halo_zero(tile + margin)
+
+    start_cols(0, 2)
+
+    @pl.when(has_up)
+    def _():
+        row_copy(0, 1).wait_recv()
+        off_copy(1).wait_recv()
+        halo_rows(0, 0)
+
+    @pl.when(jnp.logical_not(has_up))
+    def _():
+        halo_zero(0)
+
+    start_cols(0, 0)
+    gather_pass_on(0)
+
+    def take_cols(e):
+        for part in range(3):
+            @pl.when(has_left)
+            def _():
+                col_copy(e, 1, part).wait_recv()
+
+            @pl.when(has_right)
+            def _():
+                col_copy(e, 0, part).wait_recv()
+
+    def sent(e):
+        @pl.when(has_up)
+        def _():
+            row_copy(e, 0).wait_send()
+
+        @pl.when(has_down)
+        def _():
+            row_copy(e, 1).wait_send()
+
+        for part in range(3):
+            @pl.when(has_left)
+            def _():
+                col_copy(e, 0, part).wait_send()
+
+            @pl.when(has_right)
+            def _():
+                col_copy(e, 1, part).wait_send()
+
+    for side, there in ((0, has_left), (1, has_right)):
+        @pl.when(jnp.logical_not(there))
+        def _():
+            for e in range(passes + 1):
+                rcol[e, side] = jnp.zeros(rcol.shape[2:], f32)
+
+    take_cols(0)
+    for plane in range(2):
+        ext[0, plane] = acc[0, plane] + rcol[0, 0, plane]
+        ext[1, plane] = acc[1, plane]
+        ext[2, plane] = acc[2, plane] + rcol[0, 1, plane]
+    sent(0)
+
+    @pl.when(has_up)
+    def _():
+        off_copy(0).wait_send()
+
+    @pl.when(has_down)
+    def _():
+        off_copy(1).wait_send()
+
+    gather_end(0)
+
+    def probe_block(g, m, i):
+        parts = [
+            pf[g, k, pl.ds(i * pieces, pieces), m].reshape(block, pw) for k in range(n_col)
+        ]
+        return (
+            jnp.concatenate(parts[:half], 1), jnp.concatenate(parts[half:], 1)
+        )
+
+    def gradient_rows(plane, low, size):
+        return jnp.concatenate([gpad[plane, k, pl.ds(low, size), :] for k in range(2)], 1)
+
+    def unpacked(mask, values):
+        zero = jnp.zeros_like(values[:, :LANES])
+        return (
+            jnp.where(mask, values[:, :LANES], zero), values[:, LANES:],
+            jnp.where(mask, zero, values[:, :LANES]),
+        )
+
+    row_low = jnp.where(has_up, 0, margin)
+    row_high = jnp.where(has_down, extent, extent - margin)
+    col_low = jnp.where(has_left, 0, margin)
+    col_high = jnp.where(has_right, LANES, margin)
+
+    for number in range(passes):
+        outer_step, subset = number // SUBSETS, number % SUBSETS
+        g = outer_step
+        e = number + 1
+        last = e == passes
+        chosen = order_ref[subset]
+        a = pos_ref[chosen, 0]
+        b = pos_ref[chosen, 1]
+        back = lax.rem(LANES - b, LANES)
+        ahead = lax.rem(b, LANES)
+
+        @pl.loop(0, blocks)
+        def _(i):
+            rows = pl.ds(pl.multiple_of(i * block, block), block)
+            planes = []
+            for plane in range(2):
+                turned = [
+                    pltpu.roll(ext[k, plane, pl.ds(a + i * block, block), :], back, 1)
+                    for k in range(3)
+                ]
+                inside = lanes < LANES - b
+                window = jnp.concatenate(
+                    [jnp.where(inside, turned[k], turned[k + 1]) for k in range(2)], 1
+                )
+                win[plane, rows] = window
+                planes.append(window)
+            for m in range(modes):
+                p_re, p_im = probe_block(g, m, i)
+                wave = jnp.concatenate(
+                    [p_re * planes[0] - p_im * planes[1], p_re * planes[1] + p_im * planes[0]], 1
+                )
+                ew[m, rows] = wave
+                xb[m, rows] = wave.astype(jnp.bfloat16)
+
+        def transform(source, m, rows, direction, table_ref):
+            cos = jnp.dot(lt_ref[0, rows], source[m], preferred_element_type=f32)
+            sin = jnp.dot(lt_ref[1, rows], source[m], preferred_element_type=f32)
+            mixed = jnp.concatenate(
+                [
+                    cos[:, :width] + direction * sin[:, width:],
+                    cos[:, width:] - direction * sin[:, :width],
+                ],
+                1,
+            ).astype(jnp.bfloat16)
+            return jnp.dot(mixed, table_ref[...], preferred_element_type=f32)
+
+        @pl.loop(0, blocks)
+        def _(i):
+            rows = pl.ds(pl.multiple_of(i * block, block), block)
+            far = [transform(xb, m, rows, 1.0, rf_ref) for m in range(modes)]
+            intensity = sum(
+                f[:, :width] * f[:, :width] + f[:, width:] * f[:, width:] for f in far
+            )
+            scaling = meas_ref[chosen, rows] * jnp.minimum(
+                lax.rsqrt(intensity), 1.0 / amp_floor
+            )
+            scaling = jnp.concatenate([scaling, scaling], 1)
+            for m in range(modes):
+                zb[m, rows] = (far[m] * scaling).astype(jnp.bfloat16)
+
+        mask = lanes >= b
+        for i in range(blocks):
+            rows = slice(i * block, (i + 1) * block)
+            w_re, w_im = win[0, rows], win[1, rows]
+            g_re = g_im = None
+            for m in range(modes):
+                change = transform(zb, m, rows, -1.0, ri_ref) - ew[m, rows]
+                c_re, c_im = change[:, :width], change[:, width:]
+                p_re, p_im = probe_block(g, m, i)
+                part_re, part_im = p_re * c_re + p_im * c_im, p_re * c_im - p_im * c_re
+                g_re = part_re if m == 0 else g_re + part_re
+                g_im = part_im if m == 0 else g_im + part_im
+                grad = jnp.concatenate(
+                    [w_re * c_re + w_im * c_im, w_re * c_im - w_im * c_re], 1
+                )
+                at = slice(i * pieces, (i + 1) * pieces)
+                for k in range(n_col):
+                    value = grad[:, k * pw : (k + 1) * pw].reshape(pieces, pr, pw)
+                    if subset:
+                        value = value + pg[k, at, m]
+                    pg[k, at, m] = value
+            for plane, values in enumerate((g_re, g_im)):
+                first = pltpu.roll(values[:, :LANES], ahead, 1)
+                second = pltpu.roll(values[:, LANES:], ahead, 1)
+                at = slice(strip + i * block, strip + (i + 1) * block)
+                gpad[plane, 0, at] = jnp.where(mask, first, second)
+                gpad[plane, 1, at] = jnp.where(mask, second, first)
+            side = None
+            if i == 0:
+                side, there = 0, has_up
+            elif i == blocks - 1:
+                side, there = 1, has_down
+            if side is not None:
+                size = margin if last else strip
+                low = strip if side == 0 else strip + extent - size
+                for plane in range(2):
+                    srow[side, plane, 0:size] = gradient_rows(plane, low - a, size)
+
+                @pl.when(there)
+                def _():
+                    row_copy(e, side).start()
+
+        if subset == SUBSETS - 1:
+            sum_start(outer_step)
+
+        for low in (strip, 0, tile):
+            for plane in range(2):
+                parts = unpacked(mask, gradient_rows(plane, strip + low - a, strip))
+                for k in range(3):
+                    acc[k, plane, low : low + strip] = parts[k]
+            if low == strip:
+                start_cols(e, 1)
+
+        if subset == SUBSETS - 1:
+            sum_pass_on(outer_step)
+
+        def add_rows(side):
+            size = margin if last else strip
+            low = (margin if last else 0) if side == 0 else tile
+            there = roffs[side, subset, 0:1, :]
+            spot = lax.broadcasted_iota(jnp.int32, (size, LANES), 1) >= there
+            for plane in range(2):
+                parts = unpacked(spot, rrow[e, side, plane, 0:size])
+                for k in range(3):
+                    acc[k, plane, low : low + size] += parts[k]
+
+        @pl.when(has_down)
+        def _():
+            row_copy(e, 0).wait_recv()
+            add_rows(1)
+
+        start_cols(e, 2)
+
+        @pl.when(has_up)
+        def _():
+            row_copy(e, 1).wait_recv()
+            add_rows(0)
+
+        start_cols(e, 0)
+
+        if subset == SUBSETS - 1:
+            total = sum_end(outer_step)
+            piece = (prb_ref[...] if outer_step == 0 else pf[g, c, r]) + probe_rate * total
+            if last:
+                out_prb[...] = piece
+            else:
+                pf[g + 1, c, r] = piece
+                gather_send(g + 1)
+                gather_pass_on(g + 1)
+
+        take_cols(e)
+        if not last:
+            for low in range(0, extent, block):
+                row_at = lax.broadcasted_iota(jnp.int32, (block, LANES), 0) + low
+                good = jnp.logical_and(row_at >= row_low, row_at < row_high)
+                rows = slice(low, low + block)
+                for plane in range(2):
+                    for k in range(3):
+                        value = acc[k, plane, rows]
+                        kept = good
+                        if k == 0:
+                            value = value + rcol[e, 0, plane, rows]
+                            kept = jnp.logical_and(good, lanes >= col_low)
+                        elif k == 2:
+                            value = value + rcol[e, 1, plane, rows]
+                            kept = jnp.logical_and(good, lanes < col_high)
+                        ext[k, plane, rows] += jnp.where(
+                            kept, object_rate * value, jnp.zeros_like(value)
+                        )
+        else:
+            spot = lax.broadcasted_iota(jnp.int32, (margin, LANES), 1) < margin
+            for low in range(0, tile, margin):
+                rows = slice(margin + low, 2 * margin + low)
+                for plane in range(2):
+                    turned = []
+                    for k in range(3):
+                        value = acc[k, plane, rows]
+                        if k != 1:
+                            value = value + rcol[e, k // 2, plane, rows]
+                        value = ext[k, plane, rows] + object_rate * value
+                        turned.append(pltpu.roll(value, margin, 1))
+                    out_obj[plane, low : low + margin] = jnp.concatenate(
+                        [jnp.where(spot, turned[k], turned[k + 1]) for k in range(2)], 1
+                    )
+        sent(e)
+        if subset == SUBSETS - 1:
+            sum_sent(outer_step)
+            if not last:
+                gather_end(g + 1)
+
+
+def tiles(object_field, probe_modes, measured, positions, subset_order):
+    n_row, n_col = lax.axis_size("row"), lax.axis_size("col")
+    tile = object_field.shape[1]
+    modes, pr, pw = probe_modes.shape
+    pos_count, width = measured.shape[2], measured.shape[3]
+    strip = 2 * MARGIN
+    fits = (
+        pos_count == SUBSETS and strip == LANES and width == 2 * LANES and tile == width
+        and n_col % 2 == 0 and pw == LANES and pr % 8 == 0 and strip % pr == 0
+        and n_row > 1
+    )
+    if not fits:
+        return shards(object_field, probe_modes, measured, positions, subset_order)
+    extent = tile + strip
+    passes = OUTER * SUBSETS
+    half = n_col // 2
+    probe_rate = 0.5 / (pos_count * n_row * n_col)
+    left_tables, right_forward, right_inverse = host_tables(width)
+    f32, bf16 = jnp.float32, jnp.bfloat16
+    vmem = pl.BlockSpec(memory_space=pltpu.VMEM)
+    smem = pl.BlockSpec(memory_space=pltpu.SMEM)
+    copies = (passes + 1) * 8 + 2 + OUTER * n_row * 2 * n_col + OUTER * n_row * n_col
+    return pl.pallas_call(
+        functools.partial(kernel, n_row, n_col, probe_rate),
+        out_shape=(
+            jax.ShapeDtypeStruct(object_field.shape, f32),
+            jax.ShapeDtypeStruct(probe_modes.shape, f32),
+        ),
+        in_specs=[smem, smem] + [vmem] * 6,
+        out_specs=(vmem, vmem),
+        scratch_shapes=[
+            pltpu.VMEM((3, 2, extent, LANES), f32),
+            pltpu.VMEM((3, 2, extent, LANES), f32),
+            pltpu.VMEM((2, 2, width + 2 * strip, LANES), f32),
+            pltpu.VMEM((2, width, width), f32),
+            pltpu.VMEM((modes, width, 2 * width), f32),
+            pltpu.VMEM((modes, width, 2 * width), bf16),
+            pltpu.VMEM((modes, width, 2 * width), bf16),
+            pltpu.VMEM((SUBSETS, 8, LANES), jnp.int32),
+            pltpu.VMEM((2, SUBSETS, 8, LANES), jnp.int32),
+            pltpu.VMEM((2, 2, strip, width), f32),
+            pltpu.VMEM((passes + 1, 2, 2, strip, width), f32),
+            pltpu.VMEM((passes + 1, 2, 2, extent, LANES), f32),
+            pltpu.VMEM((OUTER, n_col, n_row, modes, pr, pw), f32),
+            pltpu.VMEM((n_col, n_row, modes, pr, pw), f32),
+            pltpu.VMEM((half, n_row, modes, pr, pw), f32),
+            pltpu.VMEM((OUTER, half, n_row, modes, pr, pw), f32),
+            pltpu.VMEM((OUTER, half, n_row, modes, pr, pw), f32),
+            pltpu.VMEM((n_row, modes, pr, pw), f32),
+            pltpu.VMEM((OUTER, n_row, modes, pr, pw), f32),
+            pltpu.SemaphoreType.DMA((copies,)),
+            pltpu.SemaphoreType.DMA((copies,)),
+        ],
+        compiler_params=pltpu.CompilerParams(
+            collective_id=0, has_side_effects=True, vmem_limit_bytes=48 * 1024 * 1024
+        ),
+    )(
+        positions[0, 0], subset_order[0, 0], object_field, probe_modes, measured[0, 0],
+        jnp.asarray(left_tables), jnp.asarray(right_forward), jnp.asarray(right_inverse),
+    )
+
+
 def solution(mesh):
     in_specs = (
         P(None, "row", "col"),
@@ -178,4 +795,4 @@
         P("row", "col", None),
     )
     out_specs = (P(None, "row", "col"), P(None, "row", "col"))
-    return jax.shard_map(shards, mesh=mesh, in_specs=in_specs, out_specs=out_specs, check_vma=False)
+    return jax.shard_map(tiles, mesh=mesh, in_specs=in_specs, out_specs=out_specs, check_vma=False)

time: 524 us -> 125 us (0.24); the launches traced: 516 us -> 124 us
  waiting for transfers between devices: 253 us -> 0 us
  Pallas kernels: 0 us -> 116 us
  local copies, waits for them, and re-layouts: 111 us -> 7.95 us
  starting transfers between devices: 86.1 us -> 0 us
  between operations: 27.7 us -> 0.66 us
  other arithmetic: 17.9 us -> 0 us
  blocking collectives: 11.8 us -> 0 us
  matrix products: 7.64 us -> 0 us
    unnamed x10 -> x0, waiting for transfers between devices: 149 us -> none
    pallas_call x0 -> x1, Pallas kernels: none -> 116 us  [tiles(): pl.pallas_call(functools.partial(kernel, n_row, n_col, probe_rate), out_s...]
    ppermute x32 -> x0, starting transfers between devices: 85.5 us -> none  [the longest x16 64.2 us: extended_2(): lax.ppermute(lax.slice_in_dim(block, block.shape[dim] - width, None, axis...]
    ppermute x32 -> x0, waiting for transfers between devices: 58.1 us -> none  [the longest x16 48.3 us: extended_2(): lax.ppermute(lax.slice_in_dim(block, 0, width, axis=dim), axis, backward)]
    unnamed x73 -> x18, local copies, waits for them, and re-layouts: 54.2 us -> 7.95 us
    all_gather x2 -> x0, waiting for transfers between devices: 46.2 us -> none  [spread(): return lax.all_gather(gathered, 'row', axis=1, tiled=True)]
    dynamic_update_slice x4 -> x0, local copies, waits for them, and re-layouts: 30.4 us -> none  [shards(): lax.dynamic_update_slice(grad_extended, jnp.stack([grad_re, grad_im]), st...]
    all_gather x2 -> x0, blocking collectives: 11.8 us -> none  [spread(): gathered = lax.all_gather(owned, 'col', axis=2, tiled=True)]
  transfers between devices with their start and end apart: 38 -> 0, of which waited for: 25 -> 0; matrix products, arithmetic and copies ran while one was open for 9% -> 0% of each run, Pallas kernels for 0% -> 0%
where the time goes in v1:
time: 125 us; the launch traced here: 124 us
  Pallas kernels  116 us (93%)
  local copies, waits for them, and re-layouts  7.95 us (6%)
    pallas_call x1, Pallas kernels, tiles(): pl.pallas_call(functools.partial(kernel, n_row, n_col, probe_rate), out_s...  116 us
    unnamed x18, local copies, waits for them, and re-layouts  7.95 us

profile of v1, /device:TPU:0, one launch (start us, length us, event | category | flops | bytes accessed | tf_op | source)
XLA Modules:
  0.0 124.3 jit_solution(17396044682738261734)
XLA Ops:
  0.6 0.0 copy-start.6
  0.6 0.0 copy-start.7
  0.7 0.7 copy-done.6
  1.3 0.0 copy-done.7
  1.3 0.0 copy-start
  1.3 1.0 copy-done
  2.4 0.0 copy-start.1
  2.4 1.0 copy-done.1
  3.4 0.0 copy-start.2
  3.4 1.0 copy-done.2
  4.4 0.0 copy-start.3
  4.4 1.0 copy-done.3
  5.5 0.0 copy-start.4
  5.5 0.9 copy-done.4
  6.4 0.0 copy-start.5
  6.4 0.8 copy-done.5
  7.2 115.7 %shard_map.95 = (f32[2,256,256]{2,1,0:T(8,128)S(1)}, f32[2,32,128]{2,1,0:T(8,128)S(1)}) custom-call(s32[2,2]{1,0:T(2,128)S(1)} %bitcast.4, s32[2]{0:T(128)S(1)} %bitcast.5, f32[2,256,256]{2,1,0:T(8,128)S(1)} %copy-done, f32[2,32,128]{2,1,0:T(8,128)S(1)} %copy-done.5, f32[2,256,256]{2,1,0:T(8,128)S(1)} %bitcast.3, bf16[2,256,256]{2,1,0:T(8,128)(2,1)S(1)} %copy-done.4, ...), custom_call_target="tpu_custom_call" | custom-call | tf_op jit(solution)/shard_map/pallas_call | solution.py:749
  122.9 0.8 copy.12
  123.7 0.6 copy.13
Async XLA Ops:
  0.6 0.7 copy-start.6
  0.6 0.7 copy-start.7
  1.3 1.0 copy-start
  2.4 1.0 copy-start.1
  3.4 1.0 copy-start.2
  4.4 1.0 copy-start.3
  5.5 0.9 copy-start.4
  6.4 0.8 copy-start.5

commit v2 on v1

--- a/solution.py
+++ b/solution.py
@@ -192,15 +192,16 @@
 
 def kernel(
     n_row, n_col, probe_rate,
-    pos_ref, order_ref, obj_ref, prb_ref, meas_ref, lt_ref, rf_ref, ri_ref,
+    pos_ref, order_ref, obj_far, prb_ref, meas_far, lt_far, rf_far, ri_far,
     out_obj, out_prb,
-    ext, acc, gpad, win, ew, xb, zb, offs, roffs, srow, rrow, rcol,
-    pf, pg, hs, rc, ry, ss, rr, ssem, rsem,
+    ext, acc, gpad, win, ew, xb, zb, offs, roffs, srow, rrow, rnear, rfar, rcol,
+    pf, pg, hs, rc, ry, sx, rx, ss, rr,
+    obj_ref, meas_ref, lt_ref, rf_ref, ri_ref, ssem, rsem, lsem,
 ):
     r = lax.axis_index("row")
     c = lax.axis_index("col")
-    tile = obj_ref.shape[1]
-    width = meas_ref.shape[1]
+    tile = obj_far.shape[1]
+    width = meas_far.shape[1]
     modes, pr, pw = prb_ref.shape
     margin = MARGIN
     strip = 2 * margin
@@ -226,6 +227,23 @@
             device_id=device, device_id_type=pl.DeviceIdType.MESH,
         )
 
+    nz = n_row // 2
+    z = lax.div(r, 2)
+    odd = lax.rem(r, 2)
+    pair = r + 1 - 2 * odd
+
+    loads = [
+        pltpu.make_async_copy(src, dst, lsem.at[index])
+        for index, (src, dst) in enumerate(
+            (
+                (obj_far, obj_ref), (lt_far, lt_ref), (rf_far, rf_ref), (meas_far, meas_ref),
+                (ri_far, ri_ref), (prb_ref, pf.at[0, c, r]),
+            )
+        )
+    ]
+    for load in loads:
+        load.start()
+
     barrier = pltpu.get_barrier_semaphore()
     for step in range(1, n_row):
         pl.semaphore_signal(
@@ -245,22 +263,43 @@
 
 
     def row_copy(e, side):
-        if e == 0:
-            rows = pl.ds(0, margin)
-            src = obj_ref.at[:, pl.ds(0, margin)] if side == 0 else obj_ref.at[:, pl.ds(tile - margin, margin)]
-        elif e == passes:
-            rows = pl.ds(0, margin)
-            src = srow.at[side, :, rows]
+        low = 0 if side == 0 else tile - margin
+        src = obj_far.at[:, pl.ds(low, margin)]
+        return copy(
+            ("row", e, side), src, rrow.at[1 - side], (r - 1 if side == 0 else r + 1, c)
+        )
+
+    def chunks(e):
+        return 2 if e == passes else 2 * (strip // margin)
+
+    def near_copy(e, j):
+        return copy(("near", e, j), srow.at[j], rnear.at[e - 1, j], (pair, c))
+
+    def far_copy(e, j):
+        to = jnp.where(odd == 1, r - 2, r + 2)
+        return copy(("far", e, j), rnear.at[e - 1, j], rfar.at[e - 1, j], (to, c))
+
+    even = odd == 0
+    takes_far = jnp.logical_or(
+        jnp.logical_and(even, has_up), jnp.logical_and(jnp.logical_not(even), has_down)
+    )
+    gives_far = jnp.logical_or(
+        jnp.logical_and(even, r < n_row - 2), jnp.logical_and(jnp.logical_not(even), r > 1)
+    )
+
+    def strip_low(e, part):
+        top = margin if e == passes else 0
+        if part == 0:
+            return pl.multiple_of(jnp.where(even, tile, top), margin)
+        return pl.multiple_of(jnp.where(even, top, tile), margin)
+
+    def col_copy(e, side, part):
+        if part == 1:
+            low, size = strip, tile - strip
+        elif e == 0:
+            low, size = (0, tile)[part // 2], strip
         else:
-            src = srow.at[side]
-            rows = pl.ds(0, strip)
-        dst = rrow.at[e, 1 - side, :, rows]
-        return copy(("row", e, side), src, dst, (r - 1 if side == 0 else r + 1, c))
-
-    def col_copy(e, side, part):
-        low, size = [(0, strip), (strip, tile - strip), (tile, strip)][part]
-        if e == passes:
-            low, size = [(margin, margin), (strip, tile - strip), (tile, margin)][part]
+            low, size = strip_low(e, part), margin if e == passes else strip
         rows = pl.ds(low, size)
         src = acc.at[2 * side, :, rows]
         dst = rcol.at[e, 1 - side, :, rows]
@@ -279,115 +318,164 @@
             col_copy(e, 1, part).start()
 
 
-    def ag_row(g, step):
+    def piece_at(step, other_half, sign):
+        place = 2 * lax.rem(z + (step if sign > 0 else nz - step), nz)
+        return place + (1 - odd if other_half else odd)
+
+    def own_or(g, held, step, other_half):
+        if g == 0 and step == 0 and other_half == 0:
+            return prb_ref
+        return pf.at[g, held, piece_at(step, other_half, -1)]
+
+    def ag_z(g, step):
+        to = 2 * lax.rem(z + step, nz) + odd
+        return copy(("agz", g, step), own_or(g, c, 0, 0), pf.at[g, c, r], (to, c))
+
+    def ag_x(g, step):
+        at = piece_at(step, 0, -1)
+        return copy(("agx", g, step), own_or(g, c, step, 0), pf.at[g, c, at], (pair, c))
+
+    def ag_sib(g, step, s):
+        at = piece_at(step, s, -1)
+        return copy(("ags", g, step, s), own_or(g, c, step, s), pf.at[g, c, at], (r, sibling))
+
+    def ag_par(g, step, s, other):
+        at = piece_at(step, s, -1)
+        to = 2 * lax.rem(q + other, half) + core
+        return copy(("agp", g, step, s, other), own_or(g, c, step, s), pf.at[g, c, at], (r, to))
+
+    def ag_fwd(g, step, s, other):
+        at = piece_at(step, s, -1)
+        held = 2 * lax.rem(q + half - other, half) + core
         return copy(
-            ("agr", g, step), pf.at[g, c, r], pf.at[g, c, r], (lax.rem(r + step, n_row), c)
-        )
-
-    def ag_sib(g, step):
-        at = lax.rem(r + n_row - step, n_row)
-        return copy(("ags", g, step), pf.at[g, c, at], pf.at[g, c, at], (r, sibling))
-
-    def ag_par(g, step, other):
-        at = lax.rem(r + n_row - step, n_row)
-        to = 2 * lax.rem(q + other, half) + core
-        return copy(("agp", g, step, other), pf.at[g, c, at], pf.at[g, c, at], (r, to))
-
-    def ag_fwd(g, step, other):
-        at = lax.rem(r + n_row - step, n_row)
-        held = 2 * lax.rem(q + half - other, half) + core
-        return copy(("agf", g, step, other), pf.at[g, held, at], pf.at[g, held, at], (r, sibling))
+            ("agf", g, step, s, other), pf.at[g, held, at], pf.at[g, held, at], (r, sibling)
+        )
+
+    def hand_on(g, step, s):
+        for other in range(1, half):
+            ag_par(g, step, s, other).start()
+        ag_sib(g, step, s).start()
 
     def gather_send(g):
-        for step in range(1, n_row):
-            ag_row(g, step).start()
-        ag_sib(g, 0).start()
-        for other in range(1, half):
-            ag_par(g, 0, other).start()
+        for step in range(1, nz):
+            ag_z(g, step).start()
+        ag_x(g, 0).start()
+        hand_on(g, 0, 0)
 
     def gather_pass_on(g):
-        for step in range(1, n_row):
-            ag_row(g, step).wait_recv()
-            for other in range(1, half):
-                ag_par(g, step, other).start()
-            ag_sib(g, step).start()
-        for step in range(n_row):
-            for other in range(1, half):
-                ag_par(g, step, other).wait_recv()
-                ag_fwd(g, step, other).start()
+        for step in range(1, nz):
+            ag_z(g, step).wait_recv()
+            ag_x(g, step).start()
+            hand_on(g, step, 0)
+        for step in range(nz):
+            ag_x(g, step).wait_recv()
+            hand_on(g, step, 1)
+        for s in range(2):
+            for step in range(nz):
+                for other in range(1, half):
+                    ag_par(g, step, s, other).wait_recv()
+                    ag_fwd(g, step, s, other).start()
 
     def gather_end(g):
-        for step in range(n_row):
-            ag_sib(g, step).wait_recv()
-            for other in range(1, half):
-                ag_fwd(g, step, other).wait_recv()
-        for step in range(n_row):
+        for s in range(2):
+            for step in range(nz):
+                ag_sib(g, step, s).wait_recv()
+                for other in range(1, half):
+                    ag_fwd(g, step, s, other).wait_recv()
+        for step in range(nz):
             if step:
-                ag_row(g, step).wait_send()
-            ag_sib(g, step).wait_send()
-            for other in range(1, half):
-                ag_par(g, step, other).wait_send()
-                ag_fwd(g, step, other).wait_send()
-
-
-    def rs_core(t, k):
-        return copy(("rsc", t, k), pg.at[2 * k + 1 - core], rc.at[t, k], (r, sibling))
-
-    def rs_par(t, step, other):
-        at = lax.rem(r + step, n_row)
+                ag_z(g, step).wait_send()
+            ag_x(g, step).wait_send()
+            for s in range(2):
+                ag_sib(g, step, s).wait_send()
+                for other in range(1, half):
+                    ag_par(g, step, s, other).wait_send()
+                    ag_fwd(g, step, s, other).wait_send()
+
+
+    def rs_core(t, k, i):
+        at = pl.ds(i * pieces, pieces)
+        return copy(
+            ("rsc", t, k, i), pg.at[2 * k + 1 - core, at], rc.at[t, k, at], (r, sibling)
+        )
+
+    def rs_par(t, step, s, other):
+        at = piece_at(step, s, 1)
         to_q = lax.rem(q + other, half)
         return copy(
-            ("rsp", t, step, other), hs.at[to_q, at], ry.at[t, other, at], (r, 2 * to_q + core)
-        )
-
-    def rs_row(t, step):
-        at = lax.rem(r + step, n_row)
-        return copy(("rsr", t, step), ss.at[step], rr.at[t, step], (at, c))
-
-    def sum_start(t):
+            ("rsp", t, step, s, other), hs.at[to_q, at], ry.at[t, other, at],
+            (r, 2 * to_q + core),
+        )
+
+    def rs_x(t, step):
+        return copy(("rsx", t, step), sx.at[step], rx.at[t, step], (pair, c))
+
+    def rs_z(t, step):
+        to = 2 * lax.rem(z + step, nz) + odd
+        return copy(("rsz", t, step), ss.at[step], rr.at[t, step], (to, c))
+
+    def sum_start(t, i):
         for k in range(half):
-            rs_core(t, k).start()
-
-    order = list(range(1, n_row)) + [0]
+            rs_core(t, k, i).start()
+
+    order = list(range(1, nz)) + [0]
 
     def sum_pass_on(t):
-        for k in range(half):
-            rs_core(t, k).wait_recv()
+        for i in range(blocks):
+            for k in range(half):
+                rs_core(t, k, i).wait_recv()
+        for s in (1, 0):
+            for step in order:
+                at = piece_at(step, s, 1)
+                for other in range(1, half):
+                    to_q = lax.rem(q + other, half)
+                    hs[to_q, at] = pg[2 * to_q + core, at] + rc[t, to_q, at]
+                    rs_par(t, step, s, other).start()
+
+    def sum_piece(t, step, s):
+        at = piece_at(step, s, 1)
+        value = pg[c, at] + rc[t, q, at]
+        for other in range(1, half):
+            rs_par(t, step, s, other).wait_recv()
+            value = value + ry[t, other, at]
+        return value
+
+    def sum_across(t):
         for step in order:
-            at = lax.rem(r + step, n_row)
-            for other in range(1, half):
-                to_q = lax.rem(q + other, half)
-                hs[to_q, at] = pg[2 * to_q + core, at] + rc[t, to_q, at]
-                rs_par(t, step, other).start()
+            sx[step] = sum_piece(t, step, 1)
+            rs_x(t, step).start()
         for step in order:
-            at = lax.rem(r + step, n_row)
-            value = pg[c, at] + rc[t, q, at]
-            for other in range(1, half):
-                rs_par(t, step, other).wait_recv()
-                value = value + ry[t, other, at]
-            ss[step] = value
+            value = sum_piece(t, step, 0)
+            rs_x(t, step).wait_recv()
+            ss[step] = value + rx[t, step]
             if step:
-                rs_row(t, step).start()
+                rs_z(t, step).start()
 
     def sum_end(t):
         value = ss[0]
-        for step in range(1, n_row):
-            rs_row(t, step).wait_recv()
+        for step in range(1, nz):
+            rs_z(t, step).wait_recv()
             value = value + rr[t, step]
         return value
 
     def sum_sent(t):
-        for k in range(half):
-            rs_core(t, k).wait_send()
-        for step in range(n_row):
-            for other in range(1, half):
-                rs_par(t, step, other).wait_send()
+        for i in range(blocks):
+            for k in range(half):
+                rs_core(t, k, i).wait_send()
+        for step in range(nz):
+            for s in range(2):
+                for other in range(1, half):
+                    rs_par(t, step, s, other).wait_send()
+            rs_x(t, step).wait_send()
             if step:
-                rs_row(t, step).wait_send()
+                rs_z(t, step).wait_send()
 
 
     for subset in range(SUBSETS):
-        offs[subset] = jnp.full(offs.shape[1:], pos_ref[order_ref[subset], 1], jnp.int32)
+        for d in range(2):
+            offs[subset, d] = jnp.full(
+                offs.shape[2:], pos_ref[order_ref[subset], d], jnp.int32
+            )
 
     @pl.when(has_up)
     def _():
@@ -399,8 +487,8 @@
         row_copy(0, 1).start()
         off_copy(1).start()
 
-    pf[0, c, r] = prb_ref[...]
     gather_send(0)
+    loads[0].wait()
 
     def placed(values):
         rows = values.shape[0]
@@ -425,7 +513,7 @@
 
     def halo_rows(side, at):
         for plane in range(2):
-            parts = placed(rrow[0, side, plane, 0:margin])
+            parts = placed(rrow[side, plane])
             for b in range(3):
                 acc[b, plane, at : at + margin] = parts[b]
 
@@ -470,13 +558,22 @@
                 col_copy(e, 0, part).wait_recv()
 
     def sent(e):
-        @pl.when(has_up)
-        def _():
-            row_copy(e, 0).wait_send()
-
-        @pl.when(has_down)
-        def _():
-            row_copy(e, 1).wait_send()
+        if e == 0:
+            @pl.when(has_up)
+            def _():
+                row_copy(e, 0).wait_send()
+
+            @pl.when(has_down)
+            def _():
+                row_copy(e, 1).wait_send()
+        else:
+            for j in range(chunks(e)):
+                near_copy(e, j).wait_send()
+
+            @pl.when(gives_far)
+            def _():
+                for j in range(chunks(e)):
+                    far_copy(e, j).wait_send()
 
         for part in range(3):
             @pl.when(has_left)
@@ -509,6 +606,8 @@
         off_copy(1).wait_send()
 
     gather_end(0)
+    for load in loads[1:]:
+        load.wait()
 
     def probe_block(g, m, i):
         parts = [
@@ -620,23 +719,19 @@
                 at = slice(strip + i * block, strip + (i + 1) * block)
                 gpad[plane, 0, at] = jnp.where(mask, first, second)
                 gpad[plane, 1, at] = jnp.where(mask, second, first)
-            side = None
-            if i == 0:
-                side, there = 0, has_up
-            elif i == blocks - 1:
-                side, there = 1, has_down
-            if side is not None:
-                size = margin if last else strip
-                low = strip if side == 0 else strip + extent - size
-                for plane in range(2):
-                    srow[side, plane, 0:size] = gradient_rows(plane, low - a, size)
-
-                @pl.when(there)
-                def _():
-                    row_copy(e, side).start()
-
-        if subset == SUBSETS - 1:
-            sum_start(outer_step)
+            if subset == SUBSETS - 1:
+                sum_start(outer_step, i)
+
+        for j in range(chunks(e)):
+            if last:
+                plane, top, bottom = j, 0, extent - margin
+            else:
+                plane, top = j // 2, j % 2 * margin
+                bottom = tile + top
+            srow[j] = gradient_rows(plane, strip + top - a, margin) + gradient_rows(
+                plane, strip + bottom - a, margin
+            )
+            near_copy(e, j).start()
 
         for low in (strip, 0, tile):
             for plane in range(2):
@@ -646,36 +741,47 @@
             if low == strip:
                 start_cols(e, 1)
 
+        def add_rows(part, take, arrived):
+            from_down = even if part == 0 else jnp.logical_not(even)
+            side = jnp.where(from_down, 1, 0)
+            low = strip_low(e, part)
+            there_a, there_b = roffs[side, subset, 0, 0:1, :], roffs[side, subset, 1, 0:1, :]
+            spot = lax.broadcasted_iota(jnp.int32, (margin, LANES), 1) >= there_b
+            row_at = lax.broadcasted_iota(jnp.int32, (margin, LANES), 0)
+            for j in range(chunks(e)):
+                take(e, j).wait_recv()
+                plane, top = (j, 0) if last else (j // 2, j % 2 * margin)
+                under = row_at + (margin if last else top)
+                kept = jnp.where(from_down, row_at + top - there_a, there_a - 1 - under) >= 0
+                values = arrived[e - 1, j]
+                values = jnp.where(
+                    jnp.concatenate([kept, kept], 1), values, jnp.zeros_like(values)
+                )
+                parts = unpacked(spot, values)
+                rows = pl.ds(pl.multiple_of(low + top, margin), margin)
+                for k in range(3):
+                    acc[k, plane, rows] += parts[k]
+                if part == 0:
+                    @pl.when(gives_far)
+                    def _():
+                        far_copy(e, j).start()
+
         if subset == SUBSETS - 1:
             sum_pass_on(outer_step)
-
-        def add_rows(side):
-            size = margin if last else strip
-            low = (margin if last else 0) if side == 0 else tile
-            there = roffs[side, subset, 0:1, :]
-            spot = lax.broadcasted_iota(jnp.int32, (size, LANES), 1) >= there
-            for plane in range(2):
-                parts = unpacked(spot, rrow[e, side, plane, 0:size])
-                for k in range(3):
-                    acc[k, plane, low : low + size] += parts[k]
-
-        @pl.when(has_down)
+        add_rows(0, near_copy, rnear)
+        start_cols(e, 0)
+        if subset == SUBSETS - 1:
+            sum_across(outer_step)
+
+        @pl.when(takes_far)
         def _():
-            row_copy(e, 0).wait_recv()
-            add_rows(1)
+            add_rows(2, far_copy, rfar)
 
         start_cols(e, 2)
-
-        @pl.when(has_up)
-        def _():
-            row_copy(e, 1).wait_recv()
-            add_rows(0)
-
-        start_cols(e, 0)
 
         if subset == SUBSETS - 1:
             total = sum_end(outer_step)
-            piece = (prb_ref[...] if outer_step == 0 else pf[g, c, r]) + probe_rate * total
+            piece = pf[g, c, r] + probe_rate * total
             if last:
                 out_prb[...] = piece
             else:
@@ -733,7 +839,7 @@
     fits = (
         pos_count == SUBSETS and strip == LANES and width == 2 * LANES and tile == width
         and n_col % 2 == 0 and pw == LANES and pr % 8 == 0 and strip % pr == 0
-        and n_row > 1
+        and n_row % 2 == 0
     )
     if not fits:
         return shards(object_field, probe_modes, measured, positions, subset_order)
@@ -745,14 +851,15 @@
     f32, bf16 = jnp.float32, jnp.bfloat16
     vmem = pl.BlockSpec(memory_space=pltpu.VMEM)
     smem = pl.BlockSpec(memory_space=pltpu.SMEM)
-    copies = (passes + 1) * 8 + 2 + OUTER * n_row * 2 * n_col + OUTER * n_row * n_col
+    copies = (passes + 1) * 16 + 4 + 4 * OUTER * n_row * n_col
+    far = pl.BlockSpec(memory_space=pltpu.HBM)
     return pl.pallas_call(
         functools.partial(kernel, n_row, n_col, probe_rate),
         out_shape=(
             jax.ShapeDtypeStruct(object_field.shape, f32),
             jax.ShapeDtypeStruct(probe_modes.shape, f32),
         ),
-        in_specs=[smem, smem] + [vmem] * 6,
+        in_specs=[smem, smem] + [far] * 6,
         out_specs=(vmem, vmem),
         scratch_shapes=[
             pltpu.VMEM((3, 2, extent, LANES), f32),
@@ -762,20 +869,30 @@
             pltpu.VMEM((modes, width, 2 * width), f32),
             pltpu.VMEM((modes, width, 2 * width), bf16),
             pltpu.VMEM((modes, width, 2 * width), bf16),
-            pltpu.VMEM((SUBSETS, 8, LANES), jnp.int32),
-            pltpu.VMEM((2, SUBSETS, 8, LANES), jnp.int32),
-            pltpu.VMEM((2, 2, strip, width), f32),
-            pltpu.VMEM((passes + 1, 2, 2, strip, width), f32),
+            pltpu.VMEM((SUBSETS, 2, 8, LANES), jnp.int32),
+            pltpu.VMEM((2, SUBSETS, 2, 8, LANES), jnp.int32),
+            pltpu.VMEM((4, MARGIN, width), f32),
+            pltpu.VMEM((2, 2, MARGIN, width), f32),
+            pltpu.VMEM((passes, 4, MARGIN, width), f32),
+            pltpu.VMEM((passes, 4, MARGIN, width), f32),
             pltpu.VMEM((passes + 1, 2, 2, extent, LANES), f32),
             pltpu.VMEM((OUTER, n_col, n_row, modes, pr, pw), f32),
             pltpu.VMEM((n_col, n_row, modes, pr, pw), f32),
             pltpu.VMEM((half, n_row, modes, pr, pw), f32),
             pltpu.VMEM((OUTER, half, n_row, modes, pr, pw), f32),
             pltpu.VMEM((OUTER, half, n_row, modes, pr, pw), f32),
-            pltpu.VMEM((n_row, modes, pr, pw), f32),
-            pltpu.VMEM((OUTER, n_row, modes, pr, pw), f32),
+            pltpu.VMEM((n_row // 2, modes, pr, pw), f32),
+            pltpu.VMEM((OUTER, n_row // 2, modes, pr, pw), f32),
+            pltpu.VMEM((n_row // 2, modes, pr, pw), f32),
+            pltpu.VMEM((OUTER, n_row // 2, modes, pr, pw), f32),
+            pltpu.VMEM(object_field.shape, f32),
+            pltpu.VMEM((pos_count, width, width), f32),
+            pltpu.VMEM(left_tables.shape, bf16),
+            pltpu.VMEM(right_forward.shape, bf16),
+            pltpu.VMEM(right_inverse.shape, bf16),
             pltpu.SemaphoreType.DMA((copies,)),
             pltpu.SemaphoreType.DMA((copies,)),
+            pltpu.SemaphoreType.DMA((6,)),
         ],
         compiler_params=pltpu.CompilerParams(
             collective_id=0, has_side_effects=True, vmem_limit_bytes=48 * 1024 * 1024

time: 125 us -> 120 us (0.960)
  Pallas kernels: 116 us -> 111 us
    pallas_call x1, Pallas kernels: 116 us -> 111 us  [tiles(): pl.pallas_call(functools.partial(kernel, n_row, n_col, probe_rate), out_s...]
where the time goes in v2:
time: 120 us; the launch traced here: 119 us
  Pallas kernels  111 us (92%)
  local copies, waits for them, and re-layouts  7.95 us (7%)
    pallas_call x1, Pallas kernels, tiles(): pl.pallas_call(functools.partial(kernel, n_row, n_col, probe_rate), out_s...  111 us
    unnamed x18, local copies, waits for them, and re-layouts  7.95 us

profile of v2, /device:TPU:0, one launch (start us, length us, event | category | flops | bytes accessed | tf_op | source)
XLA Modules:
  0.0 119.2 jit_solution(9026692709108400510)
XLA Ops:
  0.6 0.0 copy-start.6
  0.6 0.0 copy-start.7
  0.7 0.7 copy-done.6
  1.3 0.0 copy-done.7
  1.3 0.0 copy-start
  1.3 1.0 copy-done
  2.4 0.0 copy-start.1
  2.4 1.0 copy-done.1
  3.4 0.0 copy-start.2
  3.4 1.0 copy-done.2
  4.4 0.0 copy-start.3
  4.4 1.0 copy-done.3
  5.5 0.0 copy-start.4
  5.5 0.9 copy-done.4
  6.4 0.0 copy-start.5
  6.4 0.8 copy-done.5
  7.2 110.6 %shard_map.95 = (f32[2,256,256]{2,1,0:T(8,128)S(1)}, f32[2,32,128]{2,1,0:T(8,128)S(1)}) custom-call(s32[2,2]{1,0:T(2,128)S(1)} %bitcast.4, s32[2]{0:T(128)S(1)} %bitcast.5, f32[2,256,256]{2,1,0:T(8,128)S(1)} %copy-done, f32[2,32,128]{2,1,0:T(8,128)S(1)} %copy-done.5, f32[2,256,256]{2,1,0:T(8,128)S(1)} %bitcast.3, bf16[2,256,256]{2,1,0:T(8,128)(2,1)S(1)} %copy-done.4, ...), custom_call_target="tpu_custom_call" | custom-call | tf_op jit(solution)/shard_map/pallas_call | solution.py:856
  117.8 0.8 copy.12
  118.5 0.6 copy.13
Async XLA Ops:
  0.6 0.7 copy-start.6
  0.6 0.7 copy-start.7
  1.3 1.0 copy-start
  2.4 1.0 copy-start.1
  3.4 1.0 copy-start.2
  4.4 1.0 copy-start.3
  5.5 0.9 copy-start.4
  6.4 0.8 copy-start.5

commit v3 on v2

--- a/solution.py
+++ b/solution.py
@@ -362,14 +362,18 @@
         ag_x(g, 0).start()
         hand_on(g, 0, 0)
 
-    def gather_pass_on(g):
+    def gather_first(g):
         for step in range(1, nz):
             ag_z(g, step).wait_recv()
             ag_x(g, step).start()
             hand_on(g, step, 0)
+
+    def gather_second(g):
         for step in range(nz):
             ag_x(g, step).wait_recv()
             hand_on(g, step, 1)
+
+    def gather_third(g):
         for s in range(2):
             for step in range(nz):
                 for other in range(1, half):
@@ -440,10 +444,12 @@
             value = value + ry[t, other, at]
         return value
 
-    def sum_across(t):
+    def sum_far(t):
         for step in order:
             sx[step] = sum_piece(t, step, 1)
             rs_x(t, step).start()
+
+    def sum_near(t):
         for step in order:
             value = sum_piece(t, step, 0)
             rs_x(t, step).wait_recv()
@@ -510,6 +516,7 @@
             for b in range(3):
                 acc[b, plane, margin + low : 2 * margin + low] = parts[b]
     start_cols(0, 1)
+    gather_first(0)
 
     def halo_rows(side, at):
         for plane in range(2):
@@ -533,6 +540,7 @@
         halo_zero(tile + margin)
 
     start_cols(0, 2)
+    gather_second(0)
 
     @pl.when(has_up)
     def _():
@@ -545,7 +553,7 @@
         halo_zero(0)
 
     start_cols(0, 0)
-    gather_pass_on(0)
+    gather_third(0)
 
     def take_cols(e):
         for part in range(3):
@@ -733,6 +741,9 @@
             )
             near_copy(e, j).start()
 
+        if subset == SUBSETS - 1:
+            sum_pass_on(outer_step)
+
         for low in (strip, 0, tile):
             for plane in range(2):
                 parts = unpacked(mask, gradient_rows(plane, strip + low - a, strip))
@@ -767,11 +778,11 @@
                         far_copy(e, j).start()
 
         if subset == SUBSETS - 1:
-            sum_pass_on(outer_step)
+            sum_far(outer_step)
         add_rows(0, near_copy, rnear)
         start_cols(e, 0)
         if subset == SUBSETS - 1:
-            sum_across(outer_step)
+            sum_near(outer_step)
 
         @pl.when(takes_far)
         def _():
@@ -787,7 +798,9 @@
             else:
                 pf[g + 1, c, r] = piece
                 gather_send(g + 1)
-                gather_pass_on(g + 1)
+                gather_first(g + 1)
+                gather_second(g + 1)
+                gather_third(g + 1)
 
         take_cols(e)
         if not last:
@@ -895,7 +908,7 @@
             pltpu.SemaphoreType.DMA((6,)),
         ],
         compiler_params=pltpu.CompilerParams(
-            collective_id=0, has_side_effects=True, vmem_limit_bytes=48 * 1024 * 1024
+            collective_id=0, has_side_effects=True, vmem_limit_bytes=63 * 1024 * 1024 + 512 * 1024
         ),
     )(
         positions[0, 0], subset_order[0, 0], object_field, probe_modes, measured[0, 0],

time: 120 us -> 115 us (0.958)
  local copies, waits for them, and re-layouts: 7.95 us -> 2.49 us
    unnamed x18 -> x4, local copies, waits for them, and re-layouts: 7.95 us -> 2.49 us
where the time goes in v3:
time: 115 us; the launch traced here: 114 us
  Pallas kernels  111 us (97%)
  local copies, waits for them, and re-layouts  2.49 us (2%)
    pallas_call x1, Pallas kernels, tiles(): pl.pallas_call(functools.partial(kernel, n_row, n_col, probe_rate), out_s...  111 us
    unnamed x4, local copies, waits for them, and re-layouts  2.49 us

profile of v3, /device:TPU:0, one launch (start us, length us, event | category | flops | bytes accessed | tf_op | source)
XLA Modules:
  0.0 113.7 jit_solution(4782970241764494803)
XLA Ops:
  0.6 110.5 %shard_map.95 = (f32[2,256,256]{2,1,0:T(8,128)}, f32[2,32,128]{2,1,0:T(8,128)}) custom-call(s32[2,2]{1,0:T(2,128)} %bitcast.4, s32[2]{0:T(128)} %bitcast.5, f32[2,256,256]{2,1,0:T(8,128)} %obj_far.1, f32[2,32,128]{2,1,0:T(8,128)} %prb_ref.1, f32[2,256,256]{2,1,0:T(8,128)} %bitcast.3, bf16[2,256,256]{2,1,0:T(8,128)(2,1)} %constant.6.clone.lt_far, ...), custom_call_target="tpu_custom_call" | custom-call | tf_op jit(solution)/shard_map/pallas_call | solution.py:869
  111.2 0.0 copy-start
  111.2 1.9 %copy.12 = f32[2,256,256]{2,1,0:T(8,128)} copy(f32[2,256,256]{2,1,0:T(8,128)} %get-tuple-element.4) | data formatting | bytes 1048576
  113.1 0.0 copy-done
  113.1 0.6 copy.13
Async XLA Ops:
  111.2 1.9 %copy-start = (f32[2,32,128]{2,1,0:T(8,128)S(1)}, f32[2,32,128]{2,1,0:T(8,128)}, u32[]{:S(2)}) copy-start(f32[2,32,128]{2,1,0:T(8,128)} %get-tuple-element.5) | copy-start | bytes 98308

commit v4 on v3

--- a/solution.py
+++ b/solution.py
@@ -761,6 +761,11 @@
             row_at = lax.broadcasted_iota(jnp.int32, (margin, LANES), 0)
             for j in range(chunks(e)):
                 take(e, j).wait_recv()
+                if part == 0:
+                    @pl.when(gives_far)
+                    def _():
+                        far_copy(e, j).start()
+
                 plane, top = (j, 0) if last else (j // 2, j % 2 * margin)
                 under = row_at + (margin if last else top)
                 kept = jnp.where(from_down, row_at + top - there_a, there_a - 1 - under) >= 0
@@ -772,10 +777,6 @@
                 rows = pl.ds(pl.multiple_of(low + top, margin), margin)
                 for k in range(3):
                     acc[k, plane, rows] += parts[k]
-                if part == 0:
-                    @pl.when(gives_far)
-                    def _():
-                        far_copy(e, j).start()
 
         if subset == SUBSETS - 1:
             sum_far(outer_step)

time: 115 us -> 115 us (level)
  no operation moved by 1% of the time
where the time goes in v4:
time: 115 us; the launch traced here: 114 us
  Pallas kernels  111 us (97%)
  local copies, waits for them, and re-layouts  2.49 us (2%)
    pallas_call x1, Pallas kernels, tiles(): pl.pallas_call(functools.partial(kernel, n_row, n_col, probe_rate), out_s...  111 us
    unnamed x4, local copies, waits for them, and re-layouts  2.49 us

profile of v4, /device:TPU:0, one launch (start us, length us, event | category | flops | bytes accessed | tf_op | source)
XLA Modules:
  0.0 113.6 jit_solution(1777133341379624139)
XLA Ops:
  0.6 110.5 %shard_map.95 = (f32[2,256,256]{2,1,0:T(8,128)}, f32[2,32,128]{2,1,0:T(8,128)}) custom-call(s32[2,2]{1,0:T(2,128)} %bitcast.4, s32[2]{0:T(128)} %bitcast.5, f32[2,256,256]{2,1,0:T(8,128)} %obj_far.1, f32[2,32,128]{2,1,0:T(8,128)} %prb_ref.1, f32[2,256,256]{2,1,0:T(8,128)} %bitcast.3, bf16[2,256,256]{2,1,0:T(8,128)(2,1)} %constant.6.clone.lt_far, ...), custom_call_target="tpu_custom_call" | custom-call | tf_op jit(solution)/shard_map/pallas_call | solution.py:870
  111.1 0.0 copy-start
  111.2 1.9 %copy.12 = f32[2,256,256]{2,1,0:T(8,128)} copy(f32[2,256,256]{2,1,0:T(8,128)} %get-tuple-element.4) | data formatting | bytes 1048576
  113.0 0.0 copy-done
  113.0 0.6 copy.13
Async XLA Ops:
  111.1 1.9 %copy-start = (f32[2,32,128]{2,1,0:T(8,128)S(1)}, f32[2,32,128]{2,1,0:T(8,128)}, u32[]{:S(2)}) copy-start(f32[2,32,128]{2,1,0:T(8,128)} %get-tuple-element.5) | copy-start | bytes 98308
